TPU v7x, 32 devices: a whole 2x2x4 slice. The times are simulated.
32 devices in a mesh: grp: 2 (over x), row: 16 (over z, y, core).
Axes of the slice: x: 2, y: 2, z: 4, core: 2. Of those that a mesh axis runs over, the one named last changes fastest.
Arguments:
- coef: float32 [16384, 128], P(('grp', 'row')), parts along dimension 0, may hold values from -2 to 2
- eri: float32 [128, 3, 12, 128, 128], P(('grp', 'row')), parts along dimension 0, may hold values from -0.3125 to 0.3125
- pair_tile: int32 [128, 3], P(('grp', 'row')), parts along dimension 0, may hold values from 0 to 63, as said below
- live_count: int32 [128], P(('grp', 'row')), parts along dimension 0, may hold values from 1 to 3, as said below
Outputs:
- exchange_band: float32 [128, 5, 128, 128], P(('grp', 'row')), parts along dimension 0
There are 2 independent parts, one for each index of `grp`. A program takes and returns all parts, laid end to end along the dimension named above; each array names one. Nothing has to cross between parts.
Inputs may be any that keep to these rules, and one draw needn't show every extreme that they name: `pair_tile`: within a row the tiles are distinct and each differs from the row's own tile index by at most 2. `live_count`: some tile has all 3 slots live.
All inputs are finite; a program needn't handle non-finite values.
Results may differ from a plain program's by a relative error of at most 0.0001.
Values sent between devices are 32-bit elements; how exact they have to be, the bound alone decides.
A program may use at most 64 MiB of HBM per device.

v0:
```python
import jax
import jax.numpy as jnp
from jax import lax
from jax.sharding import PartitionSpec as P

REACH = 2


def with_halo(shard, sides, width):
    for axis, dim in sides:
        size, length = (lax.axis_size(axis), shard.shape[dim])
        up = [(i, (i + 1) % size) for i in range(size - 1)]
        down = [(j, i) for i, j in up]
        last = lax.slice_in_dim(shard, length - width, length, axis=dim)
        initial = lax.slice_in_dim(shard, 0, width, axis=dim)
        before = lax.ppermute(last, axis, up)
        after = lax.ppermute(initial, axis, down)
        shard = jnp.concatenate([before, shard, after], axis=dim)
    return shard


def passed_along(shard, axis, by):
    length = lax.axis_size(axis)
    pairs = [(i, i + by) for i in range(length) if 0 <= i + by < length]
    return lax.ppermute(shard, axis, pairs)


def contract(left, right):
    return jnp.einsum("tqmi,tqni->tmn", left, right, precision=lax.Precision.HIGHEST)


def on_device(coef, eri, pair_tile, live_count):
    tiles_dev = pair_tile.shape[0]
    pair_slots = pair_tile.shape[1]
    tile_width = eri.shape[-1]
    orbitals = coef.shape[1]
    reach = REACH
    position = lax.axis_index("row")
    extended = with_halo(coef, (("row", 0),), reach * tile_width)
    coef_tiles = extended.reshape(tiles_dev + 2 * reach, tile_width, orbitals)
    local_index = pair_tile - position * tiles_dev + reach
    picked = coef_tiles[local_index]
    alive_mask = (jnp.arange(pair_slots, dtype=jnp.int32)[None, :] < live_count[:, None]).astype(
        coef.dtype
    )
    picked = picked * alive_mask[:, :, None, None]
    half_done = jnp.einsum("tpqmn,tpni->tqmi", eri, picked, precision=lax.Precision.HIGHEST)
    from_above = passed_along(half_done[:reach], "row", -1)
    joined = jnp.concatenate([half_done, from_above], axis=0)
    upper_tiles = []
    for offset in range(reach + 1):
        upper_tiles.append(contract(half_done, joined[offset : offset + tiles_dev]))
    upper_stack = jnp.stack(upper_tiles[1:], axis=1)
    from_below = passed_along(upper_stack[tiles_dev - reach :], "row", 1)
    combined = jnp.concatenate([from_below, upper_stack], axis=0)
    lower_tiles = []
    for offset in range(reach):
        source = combined[offset : offset + tiles_dev, reach - offset - 1]
        lower_tiles.append(jnp.swapaxes(source, 1, 2))
    return jnp.stack(lower_tiles + upper_tiles, axis=1)


def solution(mesh):
    return jax.shard_map(
        on_device,
        mesh=mesh,
        in_specs=(
            P(("grp", "row"), None),
            P(("grp", "row"), None, None, None, None),
            P(("grp", "row"), None),
            P(("grp", "row")),
        ),
        out_specs=P(("grp", "row"), None, None, None),
        check_vma=False,
    )
```

profile of v0, /device:TPU:10, one launch (start us, length us, event | category | flops | bytes accessed | tf_op | source)
XLA Modules:
  0.0 79.6 jit_solution(7138886295606543112)
XLA Ops:
  0.0 1.0 %fusion.17 = (f32[256,128]{1,0:T(8,128)S(1)}, f32[256,128]{1,0:T(8,128)S(1)}) fusion(f32[512,128]{1,0:T(8,128)} %param.4), kind=kLoop, calls=%fused_computation.32 | loop fusion | bytes 524288 | tf_op jit(solution)/shard_map/slice | solution.py:14
  1.0 1.9 %collective-permute-start = (f32[256,128]{1,0:T(8,128)S(1)}, f32[256,128]{1,0:T(8,128)S(1)}, u32[]{:S(2)}, u32[]{:S(2)}) collective-permute-start(f32[256,128]{1,0:T(8,128)S(1)} %get-tuple-element.7), channel_id=1, source_target_pairs={{0,1},{1,2},{2,3},{3,4},{4,5},{5,6},{6,7},{7,8},{8,9},{9,10},{10,1... | collective-permute-start | bytes 393224 | tf_op jit(solution)/shard_map/ppermute | solution.py:16
  2.9 4.5 %collective-permute-start.1 = (f32[256,128]{1,0:T(8,128)S(1)}, f32[256,128]{1,0:T(8,128)S(1)}, u32[]{:S(2)}, u32[]{:S(2)}) collective-permute-start(f32[256,128]{1,0:T(8,128)S(1)} %get-tuple-element.8), channel_id=1, source_target_pairs={{1,0},{2,1},{3,2},{4,3},{5,4},{6,5},{7,6},{8,7},{9,8},{10,9},{11,1... | collective-permute-start | bytes 393224 | tf_op jit(solution)/shard_map/ppermute | solution.py:17
  7.5 0.7 compare_select_fusion
  8.2 0.7 fusion.14
  8.9 0.1 reshape.28
  9.0 0.0 collective-permute-done
  9.0 1.0 %collective-permute-done.1 = f32[256,128]{1,0:T(8,128)S(1)} collective-permute-done((f32[256,128]{1,0:T(8,128)S(1)}, f32[256,128]{1,0:T(8,128)S(1)}, u32[]{:S(2)}, u32[]{:S(2)}) %collective-permute-start.1) | collective-permute-done | bytes 131104 | tf_op jit(solution)/shard_map/ppermute | solution.py:17
  10.0 1.0 %pad_maximum_fusion.4 = f32[1024,128]{1,0:T(8,128)S(1)} fusion(f32[256,128]{1,0:T(8,128)S(1)} %collective-permute-done.1, f32[512,128]{1,0:T(8,128)} %param.4, f32[256,128]{1,0:T(8,128)S(1)} %collective-permute-done), kind=kLoop, calls=%fused_computation.15 | loop fusion | flops 262144 | bytes 1048576 | tf_op jit(solution)/shard_map/concatenate | solution.py:18
  11.0 0.6 gather_fusion
  11.6 1.1 %copy.5 = f32[12,128,128]{1,2,0:T(8,128)} copy(f32[12,128,128]{2,1,0:T(8,128)S(1)} %gather_fusion) | data formatting | bytes 1572864 | tf_op jit(solution)/shard_map/gather | solution.py:42
  12.7 12.5 %convolution_bitcast_fusion = f32[4,12,128,128]{2,3,1,0:T(8,128)S(1)} fusion(f32[4,3,12,128,128]{4,3,2,1,0:T(8,128)} %param.5, f32[4,3,128,128]{2,3,1,0:T(8,128)} %bitcast.48, f32[4,3]{1,0:T(4,128)S(1)} %fusion.14), kind=kOutput, calls=%fused_computation.8 | convolution fusion | flops 3624075264 | bytes 13369392 | tf_op jit(solution)/shard_map/tpqmn,tpni->tqmi/dot_general | solution.py:47
  25.2 0.1 slice.34
  25.4 4.9 %collective-permute-start.2 = (f32[2,12,128,128]{2,3,1,0:T(8,128)S(1)}, f32[2,12,128,128]{2,3,1,0:T(8,128)S(1)}, u32[]{:S(2)}, u32[]{:S(2)}) collective-permute-start(f32[2,12,128,128]{2,3,1,0:T(8,128)S(1)} %slice.34), channel_id=1, source_target_pairs={{1,0},{2,1},{3,2},{4,3},{5,4},{6,5},{7,6},{8,7},{9,8},{10,9},{11,1... | collective-permute-start | bytes 4718600 | tf_op jit(solution)/shard_map/ppermute | solution.py:25
  30.2 17.7 %collective-permute-done.2 = f32[2,12,128,128]{2,3,1,0:T(8,128)S(1)} collective-permute-done((f32[2,12,128,128]{2,3,1,0:T(8,128)S(1)}, f32[2,12,128,128]{2,3,1,0:T(8,128)S(1)}, u32[]{:S(2)}, u32[]{:S(2)}) %collective-permute-start.2) | collective-permute-done | bytes 1572896 | tf_op jit(solution)/shard_map/ppermute | solution.py:25
  48.0 5.1 %fusion.5 = f32[4,1,128,128]{3,2,0,1:T(8,128)S(1)} fusion(f32[4,12,128,128]{2,3,1,0:T(8,128)S(1)} %convolution_bitcast_fusion, f32[2,12,128,128]{2,3,1,0:T(8,128)S(1)} %collective-permute-done.2), kind=kOutput, calls=%fused_computation.9 | convolution fusion | flops 1208745984 | bytes 4980736 | tf_op jit(solution)/shard_map/tqmi,tqni->tmn/dot_general | solution.py:29
  53.1 5.1 %fusion.6 = f32[4,1,128,128]{3,2,0,1:T(8,128)S(1)} fusion(f32[4,12,128,128]{2,3,1,0:T(8,128)S(1)} %convolution_bitcast_fusion, f32[2,12,128,128]{2,3,1,0:T(8,128)S(1)} %collective-permute-done.2), kind=kOutput, calls=%fused_computation.10 | convolution fusion | flops 1208745984 | bytes 8126464 | tf_op jit(solution)/shard_map/tqmi,tqni->tmn/dot_general | solution.py:29
  58.1 0.0 copy-start
  58.2 2.1 %collective-permute-start.3 = (f32[2,2,128,128]{3,2,0,1:T(8,128)S(1)}, f32[2,2,128,128]{3,2,0,1:T(8,128)S(1)}, u32[]{:S(2)}, u32[]{:S(2)}) collective-permute-start(f32[2,2,128,128]{3,2,0,1:T(8,128)S(1)} %pad_maximum_fusion.7), channel_id=1, source_target_pairs={{0,1},{1,2},{2,3},{3,4},{4,5},{5,6},{6,7},{7,8},{8,9},{9,10},{10,1... | collective-permute-start | bytes 786440 | tf_op jit(solution)/shard_map/ppermute | solution.py:25
  60.3 6.6 %collective-permute-done.3 = f32[2,2,128,128]{3,2,0,1:T(8,128)S(1)} collective-permute-done((f32[2,2,128,128]{3,2,0,1:T(8,128)S(1)}, f32[2,2,128,128]{3,2,0,1:T(8,128)S(1)}, u32[]{:S(2)}, u32[]{:S(2)}) %collective-permute-start.3) | collective-permute-done | bytes 262176 | tf_op jit(solution)/shard_map/ppermute | solution.py:25
  66.9 0.0 copy-done
  67.0 0.8 %fusion.13 = (f32[4,1,128,128]{2,3,0,1:T(8,128)}, f32[4,1,128,128]{2,3,0,1:T(8,128)}) fusion(f32[2,2,128,128]{3,2,0,1:T(8,128)S(1)} %collective-permute-done.3, f32[4,1,128,128]{3,2,0,1:T(8,128)S(1)} %fusion.5, f32[4,1,128,128]{3,2,0,1:T(8,128)S(1)} %fusion.6), kind=kLoop, calls=%fused_computation.18 | loop fusion | flops 262144 | bytes 1310720 | tf_op jit(solution)/shard_map/stack | solution.py:60
  67.8 1.8 %copy.14 = f32[4,1,128,128]{3,2,0,1:T(8,128)} copy(f32[4,1,128,128]{2,3,0,1:T(8,128)} %get-tuple-element.5) | data formatting | bytes 524288 | tf_op jit(solution)/shard_map/stack | solution.py:60
  69.6 1.8 %copy.13 = f32[4,1,128,128]{3,2,0,1:T(8,128)} copy(f32[4,1,128,128]{2,3,0,1:T(8,128)} %get-tuple-element.6) | data formatting | bytes 524288 | tf_op jit(solution)/shard_map/stack | solution.py:60
  71.3 1.0 %constant_dynamic-update-slice_fusion.3 = f32[4,5,128,128]{3,2,0,1:T(8,128)S(1)} fusion(f32[4,1,128,128]{3,2,0,1:T(8,128)} %copy.13), kind=kLoop, calls=%fused_computation.25 | loop fusion | bytes 524288
  72.3 1.0 %constant_dynamic-update-slice_fusion.2 = f32[4,5,128,128]{3,2,0,1:T(8,128)S(1)} fusion(f32[4,5,128,128]{3,2,0,1:T(8,128)S(1)} %constant_dynamic-update-slice_fusion.3, f32[4,1,128,128]{3,2,0,1:T(8,128)} %copy.14), kind=kLoop, calls=%fused_computation.24 | loop fusion | bytes 524288
  73.3 0.0 copy-start.1
  73.3 5.1 %fusion.9 = f32[4,5,128,128]{3,2,0,1:T(8,128)S(1)} fusion(f32[4,5,128,128]{3,2,0,1:T(8,128)S(1)} %constant_dynamic-update-slice_fusion.2, f32[4,12,128,128]{2,3,1,0:T(8,128)S(1)} %convolution_bitcast_fusion), kind=kOutput, calls=%fused_computation.12 | convolution fusion | flops 1207959552 | bytes 6553600 | tf_op jit(solution)/shard_map/tqmi,tqni->tmn/dot_general | solution.py:29
  78.4 0.0 copy-done.1
  78.5 1.1 %copy.15 = f32[4,5,128,128]{3,2,1,0:T(8,128)} copy(f32[4,5,128,128]{3,2,0,1:T(8,128)S(1)} %constant_dynamic-update-slice_fusion) | data formatting | bytes 2621440 | tf_op jit(solution)/shard_map/stack | solution.py:60
  (4 shorter events, 0.1 us)
Async XLA Ops:
  1.0 8.0 %collective-permute-start = (f32[256,128]{1,0:T(8,128)S(1)}, f32[256,128]{1,0:T(8,128)S(1)}, u32[]{:S(2)}, u32[]{:S(2)}) collective-permute-start(f32[256,128]{1,0:T(8,128)S(1)} %get-tuple-element.7), channel_id=1, source_target_pairs={{0,1},{1,2},{2,3},{3,4},{4,5},{5,6},{6,7},{7,8},{8,9},{9,10},{10,1... | collective-permute-start | bytes 393224 | tf_op jit(solution)/shard_map/ppermute | solution.py:16
  2.9 7.0 %collective-permute-start.1 = (f32[256,128]{1,0:T(8,128)S(1)}, f32[256,128]{1,0:T(8,128)S(1)}, u32[]{:S(2)}, u32[]{:S(2)}) collective-permute-start(f32[256,128]{1,0:T(8,128)S(1)} %get-tuple-element.8), channel_id=1, source_target_pairs={{1,0},{2,1},{3,2},{4,3},{5,4},{6,5},{7,6},{8,7},{9,8},{10,9},{11,1... | collective-permute-start | bytes 393224 | tf_op jit(solution)/shard_map/ppermute | solution.py:17
  25.4 22.6 %collective-permute-start.2 = (f32[2,12,128,128]{2,3,1,0:T(8,128)S(1)}, f32[2,12,128,128]{2,3,1,0:T(8,128)S(1)}, u32[]{:S(2)}, u32[]{:S(2)}) collective-permute-start(f32[2,12,128,128]{2,3,1,0:T(8,128)S(1)} %slice.34), channel_id=1, source_target_pairs={{1,0},{2,1},{3,2},{4,3},{5,4},{6,5},{7,6},{8,7},{9,8},{10,9},{11,1... | collective-permute-start | bytes 4718600 | tf_op jit(solution)/shard_map/ppermute | solution.py:25
  58.1 8.8 %copy-start = (f32[4,1,128,128]{3,2,0,1:T(8,128)}, f32[4,1,128,128]{3,2,0,1:T(8,128)S(1)}, u32[]{:S(2)}) copy-start(f32[4,1,128,128]{3,2,0,1:T(8,128)S(1)} %fusion.6) | copy-start | bytes 786436
  58.2 8.8 %collective-permute-start.3 = (f32[2,2,128,128]{3,2,0,1:T(8,128)S(1)}, f32[2,2,128,128]{3,2,0,1:T(8,128)S(1)}, u32[]{:S(2)}, u32[]{:S(2)}) collective-permute-start(f32[2,2,128,128]{3,2,0,1:T(8,128)S(1)} %pad_maximum_fusion.7), channel_id=1, source_target_pairs={{0,1},{1,2},{2,3},{3,4},{4,5},{5,6},{6,7},{7,8},{8,9},{9,10},{10,1... | collective-permute-start | bytes 786440 | tf_op jit(solution)/shard_map/ppermute | solution.py:25
  73.3 5.1 %copy-start.1 = (f32[4,1,128,128]{3,2,0,1:T(8,128)S(1)}, f32[4,1,128,128]{3,2,0,1:T(8,128)}, u32[]{:S(2)}) copy-start(f32[4,1,128,128]{3,2,0,1:T(8,128)} %copy-done) | copy-start | bytes 786436
where the time goes:
time: 80 us; the launch traced here: 79.6 us
  matrix products  27.8 us (35%)
  waiting for transfers between devices  25.3 us (32%)
  starting transfers between devices  13.5 us (17%)
  local copies, waits for them, and re-layouts  9.66 us (12%)
  other arithmetic  3.25 us (4%)
    ppermute x2, waiting for transfers between devices, passed_along(): return lax.ppermute(shard, axis, pairs)  24.3 us
    dot_general x3, matrix products, contract(): jnp.einsum('tqmi,tqni->tmn', left, right, precision=lax.Precision.HIGHEST)  15.3 us
    dot_general x1, matrix products, on_device(): jnp.einsum('tpqmn,tpni->tqmi', eri, picked, precision=lax.Precision.HIGHEST)  12.5 us
    ppermute x2, starting transfers between devices, passed_along(): return lax.ppermute(shard, axis, pairs)  7 us
    another operation x4, local copies, waits for them, and re-layouts, on_device(): return jnp.stack(lower_tiles + upper_tiles, axis=1)  4.73 us
    ppermute x1, starting transfers between devices, with_halo(): after = lax.ppermute(initial, axis, down)  4.54 us
    unnamed x7, local copies, waits for them, and re-layouts  1.97 us
    ppermute x1, starting transfers between devices, with_halo(): before = lax.ppermute(last, axis, up)  1.92 us
  transfers between devices with their start and end apart: 4, of which 3 were waited for; matrix products, arithmetic and copies ran while one was open for 2% of the time, Pallas kernels for 0%

commit v1 on v0

v1 whole, which is shorter than its diff:
```python
import functools

import jax
import jax.numpy as jnp
from jax import lax
from jax.experimental import pallas as pl
from jax.experimental.pallas import tpu as pltpu
from jax.sharding import PartitionSpec as P

REACH = 2
STEP = 2
MESH = pl.DeviceIdType.MESH
F32, BF16 = jnp.float32, jnp.bfloat16


def split(x):
    high = x.astype(BF16)
    return high, (x - high.astype(F32)).astype(BF16)


def nt(left, right):
    return lax.dot_general(left, right, (((1,), (1,)), ((), ())), preferred_element_type=F32)


def kernel(
    ndev, pair_ref, live_ref, coef_ref, eri_ref, out_ref,
    cext, eri_v, parts, weights, h_hi, h_lo, snd, rcv, acc, ksnd, out_v,
    coef_sem, eri_sem, csend, crecv, hsend, hrecv, ksend, krecv, early_sem, late_sem,
):
    tiles, slots, aux, wide, _ = eri_v.shape
    orb = cext.shape[-1]
    span = slots * wide
    chunks = aux // STEP
    last = tiles - 1
    grp, row = lax.axis_index("grp"), lax.axis_index("row")
    has = (row > 0, row < ndev - 1)
    peer = ((grp, row - 1), (grp, row + 1))
    edge = (0, last)

    def remote(src, dst, send, recv, side):
        return pltpu.make_async_remote_copy(
            src_ref=src, dst_ref=dst, send_sem=send, recv_sem=recv,
            device_id=peer[side], device_id_type=MESH,
        )

    load = pltpu.make_async_copy(coef_ref, cext.at[pl.ds(REACH, tiles)], coef_sem)
    load.start()
    order = (last, 0) + tuple(range(1, last))
    loads = [pltpu.make_async_copy(eri_ref.at[t], eri_v.at[t], eri_sem.at[t]) for t in range(tiles)]
    for t in order:
        loads[t].start()

    barrier = pltpu.get_barrier_semaphore()
    for side in (0, 1):
        @pl.when(has[side])
        def _():
            pl.semaphore_signal(barrier, inc=1, device_id=peer[side], device_id_type=MESH)
    pl.semaphore_wait(barrier, has[0].astype(jnp.int32) + has[1].astype(jnp.int32))
    load.wait()

    def coef_copy(side):
        src = (REACH, tiles)[side]
        dst = (REACH + tiles, 0)[side]
        return remote(
            cext.at[pl.ds(src, REACH)], cext.at[pl.ds(dst, REACH)],
            csend.at[side], crecv.at[1 - side], side,
        )

    for side in (1, 0):
        @pl.when(has[side])
        def _():
            coef_copy(side).start()

        @pl.when(jnp.logical_not(has[side]))
        def _():
            rcv[side] = jnp.zeros(rcv.shape[1:], F32)
            cext[pl.ds((0, REACH + tiles)[side], REACH)] = jnp.zeros((REACH, wide, orb), F32)
            out_v[edge[side], (0, 2 * REACH)[side]] = jnp.zeros((wide, wide), F32)

    def split_eri(t):
        loads[t].wait()

        def body(q, carry):
            for p in range(slots):
                high, low = split(eri_v[t, p, q])
                parts[t, q, :, p * wide:(p + 1) * wide] = high
                parts[t, q, :, span + p * wide:span + (p + 1) * wide] = low
            return carry

        lax.fori_loop(0, aux, body, 0)

    def pick(t):
        live = live_ref[t]
        for p in range(slots):
            index = jnp.clip(pair_ref[t, p] - row * tiles + REACH, 0, tiles + 2 * REACH - 1)
            high, low = split(jnp.where(p < live, cext[index], 0.0))
            both = jnp.concatenate([high, low], axis=1)
            weights[t, p * wide:(p + 1) * wide, :] = both
            weights[t, span + p * wide:span + (p + 1) * wide, :] = both

    def half(t, first, count, side=None):
        left = parts[t, first:first + count].reshape(count * wide, 2 * span)
        both = jnp.dot(left, weights[t], preferred_element_type=F32)
        block = both[:, :orb] + both[:, orb:]
        for k in range(count):
            x = block[k * wide:(k + 1) * wide]
            high, low = split(x)
            rows, cols = slice(t * wide, (t + 1) * wide), slice((first + k) * orb, (first + k + 1) * orb)
            h_hi[rows, cols] = high
            h_lo[rows, cols] = low
            if side is not None:
                snd[side, first + k] = x

    split_eri(last)
    split_eri(0)
    for side in (0, 1):
        @pl.when(has[side])
        def _():
            coef_copy(1 - side).wait_recv()
    pick(last)
    pick(0)

    def half_copy(side, c):
        piece = pl.ds(c * STEP, STEP)
        return remote(
            snd.at[side, piece], rcv.at[1 - side, piece],
            hsend.at[side, c], hrecv.at[1 - side, c], side,
        )

    for c in range(chunks):
        for side in (1, 0):
            half(edge[side], c * STEP, STEP, side)

            @pl.when(has[side])
            def _():
                half_copy(side, c).start()

    for t in range(1, last):
        split_eri(t)
        pick(t)
        for c in range(2):
            half(t, c * (aux // 2), aux // 2)

    for first in range(0, tiles, 2):
        rows = pl.ds(first * wide, 2 * wide)
        gram = nt(h_hi[...], h_hi[rows, :]) + nt(h_lo[...], h_hi[rows, :]) + nt(h_hi[...], h_lo[rows, :])
        for other in (first, first + 1):
            for t in range(max(0, other - REACH), min(tiles, other + REACH + 1)):
                col = (other - first) * wide
                out_v[t, other - t + REACH] = gram[t * wide:(t + 1) * wide, col:col + wide]

    early = []
    for t in range(tiles):
        low, high = max(0, REACH - t), min(2 * REACH, tiles - 1 - t + REACH)
        piece = pl.ds(low, high - low + 1)
        early.append(pltpu.make_async_copy(out_v.at[t, piece], out_ref.at[t, piece], early_sem.at[t]))
        early[-1].start()

    acc[...] = jnp.zeros_like(acc)
    near = (pl.ds(0, 2 * wide), pl.ds((tiles - 2) * wide, 2 * wide))
    for c in range(chunks):
        for side in (0, 1):
            @pl.when(has[side])
            def _():
                half_copy(1 - side, c).wait_recv()
            cols = pl.ds(c * STEP * orb, STEP * orb)
            x = jnp.concatenate([rcv[side, c * STEP + k] for k in range(STEP)], axis=1)
            high, low = split(x)
            mine = h_hi[near[side], cols]
            acc[side] += nt(high, mine) + nt(low, mine) + nt(high, h_lo[near[side], cols])

    far = (slice(wide, 2 * wide), slice(0, wide))
    close = (slice(0, wide), slice(wide, 2 * wide))
    far_tile = (1, tiles - 2)
    far_at = (0, 2 * REACH)

    def k_copy(side):
        return remote(
            ksnd.at[side], out_ref.at[edge[1 - side], far_at[1 - side]],
            ksend.at[side], krecv.at[1 - side], side,
        )

    late = []
    for side in (0, 1):
        ksnd[side] = acc[side, :, far[side]]

        @pl.when(has[side])
        def _():
            k_copy(side).start()
    for side in (0, 1):
        out_v[far_tile[side], far_at[side]] = acc[side, :, far[side]].T
        out_v[edge[side], (1, 3)[side]] = acc[side, :, close[side]].T
        for n, (t, o) in enumerate(((far_tile[side], far_at[side]), (edge[side], (1, 3)[side]))):
            late.append(pltpu.make_async_copy(out_v.at[t, o], out_ref.at[t, o], late_sem.at[side, n]))
            late[-1].start()

        @pl.when(jnp.logical_not(has[side]))
        def _():
            fill = pltpu.make_async_copy(
                out_v.at[edge[side], far_at[side]], out_ref.at[edge[side], far_at[side]], krecv.at[side]
            )
            fill.start()
            fill.wait()

    for copy in early + late:
        copy.wait()
    for side in (0, 1):
        @pl.when(has[side])
        def _():
            coef_copy(side).wait_send()
            for c in range(chunks):
                half_copy(side, c).wait_send()
            k_copy(side).wait_send()
            k_copy(1 - side).wait_recv()


def on_device(ndev, coef, eri, pair_tile, live_count):
    tiles, slots, aux, wide, _ = eri.shape
    orb = coef.shape[1]
    chunks = aux // STEP
    dma = pltpu.SemaphoreType.DMA
    flops = 2 * 3 * tiles * aux * wide * wide * orb * (slots + 2 * REACH + 1)
    return pl.pallas_call(
        functools.partial(kernel, ndev),
        out_shape=jax.ShapeDtypeStruct((tiles, 2 * REACH + 1, wide, wide), F32),
        in_specs=[
            pl.BlockSpec(memory_space=pltpu.SMEM),
            pl.BlockSpec(memory_space=pltpu.SMEM),
            pl.BlockSpec(memory_space=pl.ANY),
            pl.BlockSpec(memory_space=pl.ANY),
        ],
        out_specs=pl.BlockSpec(memory_space=pl.ANY),
        scratch_shapes=[
            pltpu.VMEM((tiles + 2 * REACH, wide, orb), F32),
            pltpu.VMEM(eri.shape, F32),
            pltpu.VMEM((tiles, aux, wide, 2 * slots * wide), BF16),
            pltpu.VMEM((tiles, 2 * slots * wide, 2 * orb), BF16),
            pltpu.VMEM((tiles * wide, aux * orb), BF16),
            pltpu.VMEM((tiles * wide, aux * orb), BF16),
            pltpu.VMEM((2, aux, wide, orb), F32),
            pltpu.VMEM((2, aux, wide, orb), F32),
            pltpu.VMEM((2, wide, 2 * wide), F32),
            pltpu.VMEM((2, wide, wide), F32),
            pltpu.VMEM((tiles, 2 * REACH + 1, wide, wide), F32),
            dma(()), dma((tiles,)), dma((2,)), dma((2,)), dma((2, chunks)), dma((2, chunks)),
            dma((2,)), dma((2,)), dma((tiles,)), dma((2, 2)),
        ],
        compiler_params=pltpu.CompilerParams(
            collective_id=0, has_side_effects=True, vmem_limit_bytes=50 * 2**20
        ),
        cost_estimate=pl.CostEstimate(
            flops=flops, bytes_accessed=4 * eri.size, transcendentals=0
        ),
    )(pair_tile, live_count, coef.reshape(tiles, wide, orb), eri)


def solution(mesh):
    return jax.shard_map(
        functools.partial(on_device, mesh.shape["row"]),
        mesh=mesh,
        in_specs=(
            P(("grp", "row"), None),
            P(("grp", "row"), None, None, None, None),
            P(("grp", "row"), None),
            P(("grp", "row")),
        ),
        out_specs=P(("grp", "row"), None, None, None),
        check_vma=False,
    )
```

time: 80 us -> 34 us (0.42)
  the two profiles are of different devices: /device:TPU:10 before, /device:TPU:9 now
where the time goes in v1:
time: 34 us; the launch traced here: 33.8 us
  Pallas kernels  30.5 us (90%)
  local copies, waits for them, and re-layouts  3.34 us (10%)
    pallas_call x1, Pallas kernels, on_device(): pl.pallas_call(functools.partial(kernel, ndev), out_shape=jax.ShapeDtypeS...  30.5 us
    unnamed x7, local copies, waits for them, and re-layouts  3.34 us

profile of v1, /device:TPU:9, one launch (start us, length us, event | category | flops | bytes accessed | tf_op | source)
XLA Modules:
  0.0 33.8 jit_solution(5475256724631079188)
XLA Ops:
  0.0 0.0 copy-start
  0.0 0.9 %copy-done = f32[512,128]{1,0:T(8,128)S(1)} copy-done((f32[512,128]{1,0:T(8,128)S(1)}, f32[512,128]{1,0:T(8,128)}, u32[]{:S(2)}) %copy-start) | copy-done | bytes 262168
  1.0 0.0 copy-start.1
  1.0 0.7 %copy-done.1 = s32[4,3]{1,0:T(4,128)S(1)} copy-done((s32[4,3]{1,0:T(4,128)S(1)}, s32[4,3]{1,0:T(4,128)}, u32[]{:S(2)}) %copy-start.1) | copy-done | bytes 72
  1.6 0.0 copy-start.2
  1.6 0.7 %copy-done.2 = s32[4]{0:T(128)S(1)} copy-done((s32[4]{0:T(128)S(1)}, s32[4]{0:T(128)}, u32[]{:S(2)}) %copy-start.2) | copy-done | bytes 40
  2.3 30.5 %shard_map.46 = f32[4,5,128,128]{3,2,1,0:T(8,128)S(1)} custom-call(s32[4,3]{1,0:T(4,128)S(1)} %copy-done.1, s32[4]{0:T(128)S(1)} %copy-done.2, f32[4,128,128]{2,1,0:T(8,128)S(1)} %bitcast.1, f32[4,3,12,128,128]{4,3,2,1,0:T(8,128)} %eri_ref.1), custom_call_target="tpu_custom_call" | custom-call | flops 4831838208 | bytes 9437184 | tf_op jit(solution)/shard_map/pallas_call | solution.py:223
  32.8 1.1 %copy.6 = f32[4,5,128,128]{3,2,1,0:T(8,128)} copy(f32[4,5,128,128]{3,2,1,0:T(8,128)S(1)} %shard_map.46) | data formatting | bytes 2621440
Async XLA Ops:
  0.0 0.9 %copy-start = (f32[512,128]{1,0:T(8,128)S(1)}, f32[512,128]{1,0:T(8,128)}, u32[]{:S(2)}) copy-start(f32[512,128]{1,0:T(8,128)} %param.4) | copy-start | bytes 786436
  1.0 0.7 %copy-start.1 = (s32[4,3]{1,0:T(4,128)S(1)}, s32[4,3]{1,0:T(4,128)}, u32[]{:S(2)}) copy-start(s32[4,3]{1,0:T(4,128)} %pair_ref.1) | copy-start | bytes 148
  1.6 0.7 %copy-start.2 = (s32[4]{0:T(128)S(1)}, s32[4]{0:T(128)}, u32[]{:S(2)}) copy-start(s32[4]{0:T(128)} %live_ref.1) | copy-start | bytes 52

commit v2 on v1

--- a/solution.py
+++ b/solution.py
@@ -9,6 +9,7 @@
 
 REACH = 2
 STEP = 2
+DEPTH = 2
 MESH = pl.DeviceIdType.MESH
 F32, BF16 = jnp.float32, jnp.bfloat16
 
@@ -23,9 +24,9 @@
 
 
 def kernel(
-    ndev, pair_ref, live_ref, coef_ref, eri_ref, out_ref,
-    cext, eri_v, parts, weights, h_hi, h_lo, snd, rcv, acc, ksnd, out_v,
-    coef_sem, eri_sem, csend, crecv, hsend, hrecv, ksend, krecv, early_sem, late_sem,
+    ndev, pair_hbm, live_hbm, coef_ref, eri_ref, out_ref,
+    pair_ref, live_ref, cext, eri_v, parts, weights, h_hi, h_lo, snd, rcv, acc, ksnd, out_v,
+    index_sem, coef_sem, eri_sem, csend, crecv, hsend, hrecv, ksend, krecv, early_sem, late_sem,
 ):
     tiles, slots, aux, wide, _ = eri_v.shape
     orb = cext.shape[-1]
@@ -45,6 +46,12 @@
 
     load = pltpu.make_async_copy(coef_ref, cext.at[pl.ds(REACH, tiles)], coef_sem)
     load.start()
+    small = (
+        pltpu.make_async_copy(pair_hbm, pair_ref, index_sem.at[0]),
+        pltpu.make_async_copy(live_hbm, live_ref, index_sem.at[1]),
+    )
+    for copy in small:
+        copy.start()
     order = (last, 0) + tuple(range(1, last))
     loads = [pltpu.make_async_copy(eri_ref.at[t], eri_v.at[t], eri_sem.at[t]) for t in range(tiles)]
     for t in order:
@@ -113,6 +120,8 @@
 
     split_eri(last)
     split_eri(0)
+    for copy in small:
+        copy.wait()
     for side in (0, 1):
         @pl.when(has[side])
         def _():
@@ -127,19 +136,30 @@
             hsend.at[side, c], hrecv.at[1 - side, c], side,
         )
 
-    for c in range(chunks):
+    def pump(c):
+        for side in (1, 0):
+            @pl.when(has[side])
+            def _():
+                if c >= DEPTH:
+                    half_copy(side, c - DEPTH).wait_send()
+                half_copy(side, c).start()
+
+    for c in range(DEPTH):
         for side in (1, 0):
             half(edge[side], c * STEP, STEP, side)
-
-            @pl.when(has[side])
-            def _():
-                half_copy(side, c).start()
-
-    for t in range(1, last):
+        pump(c)
+    done = DEPTH * STEP
+    for side in (1, 0):
+        half(edge[side], done, aux - done, side)
+
+    split_eri(1)
+    pick(1)
+    half(1, 0, aux)
+    pump(DEPTH)
+    for t in range(2, last):
         split_eri(t)
         pick(t)
-        for c in range(2):
-            half(t, c * (aux // 2), aux // 2)
+        half(t, 0, aux)
 
     for first in range(0, tiles, 2):
         rows = pl.ds(first * wide, 2 * wide)
@@ -148,6 +168,8 @@
             for t in range(max(0, other - REACH), min(tiles, other + REACH + 1)):
                 col = (other - first) * wide
                 out_v[t, other - t + REACH] = gram[t * wide:(t + 1) * wide, col:col + wide]
+        if first == 0:
+            pump(DEPTH + 1)
 
     early = []
     for t in range(tiles):
@@ -159,6 +181,8 @@
     acc[...] = jnp.zeros_like(acc)
     near = (pl.ds(0, 2 * wide), pl.ds((tiles - 2) * wide, 2 * wide))
     for c in range(chunks):
+        if c + DEPTH + 2 < chunks:
+            pump(c + DEPTH + 2)
         for side in (0, 1):
             @pl.when(has[side])
             def _():
@@ -167,7 +191,8 @@
             x = jnp.concatenate([rcv[side, c * STEP + k] for k in range(STEP)], axis=1)
             high, low = split(x)
             mine = h_hi[near[side], cols]
-            acc[side] += nt(high, mine) + nt(low, mine) + nt(high, h_lo[near[side], cols])
+            both = nt(jnp.concatenate([high, low], axis=0), mine)
+            acc[side] += both[:wide] + both[wide:] + nt(high, h_lo[near[side], cols])
 
     far = (slice(wide, 2 * wide), slice(0, wide))
     close = (slice(0, wide), slice(wide, 2 * wide))
@@ -208,7 +233,7 @@
         @pl.when(has[side])
         def _():
             coef_copy(side).wait_send()
-            for c in range(chunks):
+            for c in range(chunks - DEPTH, chunks):
                 half_copy(side, c).wait_send()
             k_copy(side).wait_send()
             k_copy(1 - side).wait_recv()
@@ -224,13 +249,15 @@
         functools.partial(kernel, ndev),
         out_shape=jax.ShapeDtypeStruct((tiles, 2 * REACH + 1, wide, wide), F32),
         in_specs=[
-            pl.BlockSpec(memory_space=pltpu.SMEM),
-            pl.BlockSpec(memory_space=pltpu.SMEM),
-            pl.BlockSpec(memory_space=pl.ANY),
-            pl.BlockSpec(memory_space=pl.ANY),
+            pl.BlockSpec(memory_space=pltpu.HBM),
+            pl.BlockSpec(memory_space=pltpu.HBM),
+            pl.BlockSpec(memory_space=pltpu.HBM),
+            pl.BlockSpec(memory_space=pltpu.HBM),
         ],
         out_specs=pl.BlockSpec(memory_space=pl.ANY),
         scratch_shapes=[
+            pltpu.SMEM(pair_tile.shape, jnp.int32),
+            pltpu.SMEM(live_count.shape, jnp.int32),
             pltpu.VMEM((tiles + 2 * REACH, wide, orb), F32),
             pltpu.VMEM(eri.shape, F32),
             pltpu.VMEM((tiles, aux, wide, 2 * slots * wide), BF16),
@@ -242,7 +269,7 @@
             pltpu.VMEM((2, wide, 2 * wide), F32),
             pltpu.VMEM((2, wide, wide), F32),
             pltpu.VMEM((tiles, 2 * REACH + 1, wide, wide), F32),
-            dma(()), dma((tiles,)), dma((2,)), dma((2,)), dma((2, chunks)), dma((2, chunks)),
+            dma((2,)), dma(()), dma((tiles,)), dma((2,)), dma((2,)), dma((2, chunks)), dma((2, chunks)),
             dma((2,)), dma((2,)), dma((tiles,)), dma((2, 2)),
         ],
         compiler_params=pltpu.CompilerParams(

time: 34 us -> 32.6 us (0.959)
  Pallas kernels: 30.5 us -> 29.1 us
    pallas_call x1, Pallas kernels: 30.5 us -> 29.1 us  [on_device(): pl.pallas_call(functools.partial(kernel, ndev), out_shape=jax.ShapeDtypeS...]
where the time goes in v2:
time: 32.6 us; the launch traced here: 32.4 us
  Pallas kernels  29.1 us (89%)
  local copies, waits for them, and re-layouts  3.34 us (10%)
    pallas_call x1, Pallas kernels, on_device(): pl.pallas_call(functools.partial(kernel, ndev), out_shape=jax.ShapeDtypeS...  29.1 us
    unnamed x7, local copies, waits for them, and re-layouts  3.34 us

profile of v2, /device:TPU:9, one launch (start us, length us, event | category | flops | bytes accessed | tf_op | source)
XLA Modules:
  0.0 32.4 jit_solution(3763554008595248194)
XLA Ops:
  0.0 0.0 copy-start
  0.0 0.9 %copy-done = f32[512,128]{1,0:T(8,128)S(1)} copy-done((f32[512,128]{1,0:T(8,128)S(1)}, f32[512,128]{1,0:T(8,128)}, u32[]{:S(2)}) %copy-start) | copy-done | bytes 262168
  1.0 0.0 copy-start.1
  1.0 0.7 %copy-done.1 = s32[4,3]{1,0:T(4,128)S(1)} copy-done((s32[4,3]{1,0:T(4,128)S(1)}, s32[4,3]{1,0:T(4,128)}, u32[]{:S(2)}) %copy-start.1) | copy-done | bytes 72
  1.6 0.0 copy-start.2
  1.6 0.7 %copy-done.2 = s32[4]{0:T(128)S(1)} copy-done((s32[4]{0:T(128)S(1)}, s32[4]{0:T(128)}, u32[]{:S(2)}) %copy-start.2) | copy-done | bytes 40
  2.3 29.1 %shard_map.46 = f32[4,5,128,128]{3,2,1,0:T(8,128)S(1)} custom-call(s32[4,3]{1,0:T(4,128)S(1)} %copy-done.1, s32[4]{0:T(128)S(1)} %copy-done.2, f32[4,128,128]{2,1,0:T(8,128)S(1)} %bitcast.1, f32[4,3,12,128,128]{4,3,2,1,0:T(8,128)} %eri_ref.1), custom_call_target="tpu_custom_call" | custom-call | flops 4831838208 | bytes 9437184 | tf_op jit(solution)/shard_map/pallas_call | solution.py:248
  31.4 1.1 %copy.6 = f32[4,5,128,128]{3,2,1,0:T(8,128)} copy(f32[4,5,128,128]{3,2,1,0:T(8,128)S(1)} %shard_map.46) | data formatting | bytes 2621440
Async XLA Ops:
  0.0 0.9 %copy-start = (f32[512,128]{1,0:T(8,128)S(1)}, f32[512,128]{1,0:T(8,128)}, u32[]{:S(2)}) copy-start(f32[512,128]{1,0:T(8,128)} %param.4) | copy-start | bytes 786436
  1.0 0.7 %copy-start.1 = (s32[4,3]{1,0:T(4,128)S(1)}, s32[4,3]{1,0:T(4,128)}, u32[]{:S(2)}) copy-start(s32[4,3]{1,0:T(4,128)} %pair_hbm.1) | copy-start | bytes 148
  1.6 0.7 %copy-start.2 = (s32[4]{0:T(128)S(1)}, s32[4]{0:T(128)}, u32[]{:S(2)}) copy-start(s32[4]{0:T(128)} %live_hbm.1) | copy-start | bytes 52
